TPU v7x, 512 devices: a whole 4x8x8 slice. The times are simulated.
512 devices in a mesh: rec: 16 (over z, core), frame: 32 (over x, y).
Axes of the slice: x: 4, y: 8, z: 8, core: 2. Of those that a mesh axis runs over, the one named last changes fastest.
Arguments:
- frames: bfloat16 [16, 49152, 256], P('rec', 'frame'), may hold values from -10 to 10
- texts: bfloat16 [32, 224, 256], P('rec', 'frame'), may hold values from -100 to 100
- pair_rec: int32 [32, 1], replicated, may hold values from 0 to 15, as said below
- pair_text: int32 [32], replicated, may hold values from 0 to 31, as said below
- pair_label: int32 [32], replicated, may hold values 0 or 1
Outputs:
- loss: float32 [], replicated
- grad_frames: bfloat16 [16, 49152, 256], P('rec', 'frame')
- grad_texts: bfloat16 [32, 224, 256], P('rec', 'frame')
Inputs may be any that keep to these rules, and one draw needn't show every extreme that they name: `pair_rec`: no recording is named by more than 6 pairs, some recording by exactly 6, and every recording by at least one. A pair's text is held by the index of rec one after, one before, or 8 after its recording (counted round): pair_text // 2 = (pair_rec + k) mod 16 with k one of 1, 15, 8.
All inputs are finite; a program needn't handle non-finite values.
Results may differ from a plain program's by a relative error of at most 0.0085.
Values may be sent and summed in bfloat16 or wider, within the bound.
A program may use at most 64 MiB of HBM per device.

v0:
```python
import jax
import jax.numpy as jnp
from jax import lax
from jax.sharding import PartitionSpec as P

MOST = 6


EPS = 1e-06
TEMP = 10.0
BIAS = -1.0
LOSS_SCALE = 2048.0


def slot_tables(pair_rec, pair_text, pair_label, here, most):
    record = pair_rec[:, 0]
    count = record.shape[0]
    order = jnp.arange(count, dtype=jnp.int32)
    same = (record[:, None] == record[None, :]).astype(jnp.int32)
    earlier = (order[None, :] < order[:, None]).astype(jnp.int32)
    rank = jnp.sum(same * earlier, axis=1)
    places = jnp.arange(most, dtype=jnp.int32)
    chosen = ((record[None, :] == here) & (rank[None, :] == places[:, None])).astype(jnp.int32)
    valid = jnp.sum(chosen, axis=1)
    slot_text = jnp.sum(chosen * pair_text[None, :], axis=1)
    sign = jnp.sum(chosen * (2 * pair_label[None, :] - 1), axis=1)
    return (valid, slot_text, sign)


def pair_terms(score, valid, sign, tokens):
    margin = -sign * (TEMP * score + BIAS)
    loss_part = valid * jax.nn.softplus(margin)
    grad_cos = -LOSS_SCALE * TEMP * valid * sign * jax.nn.sigmoid(margin) / tokens
    return (loss_part, grad_cos)


def body(frames, texts, pair_rec, pair_text, pair_label):
    here = lax.axis_index("rec")
    part = lax.axis_index("frame")
    owned, width_rows, width = texts.shape
    tokens = width_rows * lax.axis_size("frame")
    n_text = owned * lax.axis_size("rec")
    valid, slot_text, sign = slot_tables(pair_rec, pair_text, pair_label, here, MOST)
    valid_f = valid.astype(jnp.float32)
    sign_f = sign.astype(jnp.float32)
    picks = (
        (slot_text[:, None] == jnp.arange(n_text, dtype=jnp.int32)[None, :]) & (valid[:, None] > 0)
    ).astype(jnp.bfloat16)
    whole = lax.all_gather(texts, "frame", axis=1, tiled=True)
    query_vectors = jnp.einsum(
        "jc,cgx->jgx",
        picks,
        lax.all_gather(whole, "rec", axis=0, tiled=True),
        preferred_element_type=jnp.float32,
    ).astype(jnp.bfloat16)
    upstream_signal = frames[0]
    logit_scale = width ** (-0.5)
    pair_scores = (
        jnp.einsum(
            "ype,je->ypj", query_vectors, upstream_signal, preferred_element_type=jnp.float32
        )
        * logit_scale
    )
    local_max = jnp.max(pair_scores, axis=2)
    row_max = lax.pmax(local_max, "frame")
    expo = jnp.exp(pair_scores - row_max[..., None])
    batch_weights = expo.astype(jnp.bfloat16)
    value_partial = jnp.einsum(
        "pqx,xh->pqh", batch_weights, upstream_signal, preferred_element_type=jnp.float32
    )
    query_f = query_vectors.astype(jnp.float32)
    q_norm = lax.rsqrt(jnp.sum(query_f * query_f, axis=2) + EPS)
    q_unit = query_f * q_norm[..., None]
    context = lax.psum(value_partial, "frame")
    c_norm = lax.rsqrt(jnp.sum(context * context, axis=2) + EPS)
    c_unit = context * c_norm[..., None]
    cos = jnp.sum(q_unit * c_unit, axis=2)
    score = jnp.mean(cos, axis=1)
    loss_part, grad_cos = pair_terms(score, valid_f, sign_f, tokens)
    weight = grad_cos[:, None, None]
    d_context = weight * (q_unit - cos[..., None] * c_unit) * c_norm[..., None]
    direct = weight * (c_unit - cos[..., None] * q_unit) * q_norm[..., None]
    direct_own = lax.dynamic_slice_in_dim(direct, part * width_rows, width_rows, 1)
    context_batch_gradient = d_context.astype(jnp.bfloat16)
    weight_gradient = jnp.einsum(
        "ype,je->ypj", context_batch_gradient, upstream_signal, preferred_element_type=jnp.float32
    )
    score_gradient = (expo * weight_gradient * logit_scale).astype(jnp.bfloat16)
    d_query = lax.psum_scatter(
        jnp.einsum(
            "slf,fd->lsd", score_gradient, upstream_signal, preferred_element_type=jnp.float32
        ),
        "frame",
        scatter_dimension=0,
        tiled=True,
    )
    d_query = d_query + jnp.transpose(direct_own, (1, 0, 2))
    text_term = jnp.einsum(
        "st,lsd->tld", picks.astype(jnp.float32), d_query, precision=lax.Precision.HIGHEST
    )
    grad_texts = lax.psum_scatter(text_term, "rec", scatter_dimension=0, tiled=True).astype(
        jnp.bfloat16
    )
    frame_loss_piece = jnp.einsum(
        "cvm,cvz->mz", score_gradient, query_vectors, preferred_element_type=jnp.float32
    )
    frame_loss_piece = frame_loss_piece + jnp.einsum(
        "cvm,cvz->mz", batch_weights, context_batch_gradient, preferred_element_type=jnp.float32
    )
    grad_frames = frame_loss_piece.astype(jnp.bfloat16)[None]
    loss = lax.psum(jnp.sum(loss_part), "rec")
    return (loss, grad_frames, grad_texts)


def solution(mesh):
    return jax.shard_map(
        body,
        mesh=mesh,
        in_specs=(P("rec", "frame", None), P("rec", "frame", None), P(), P(), P()),
        out_specs=(P(), P("rec", "frame", None), P("rec", "frame", None)),
        check_vma=False,
    )
```

profile of v0, /device:TPU:1, one launch (start us, length us, event | category | flops | bytes accessed | tf_op | source)
XLA Modules:
  0.0 642.6 jit_solution(15901261809968272552)
XLA Ops:
  7.2 38.8 %all_gather.6 = bf16[2,224,256]{2,0,1:T(2,128)(2,1)S(1)} all-gather(bf16[2,7,256]{2,0,1:T(2,128)(2,1)} %param.6), channel_id=1, replica_groups=mesh['rec'=16,'frame'=32] {'frame'}, dimensions={1}, use_global_device_ids=true | all-gather | bytes 236544 | tf_op jit(solution)/shard_map/all_gather | solution.py:49
  46.1 0.7 copy.20
  46.9 0.9 select_reduce_fusion
  47.8 0.7 broadcast_compare_fusion.1
  48.4 0.7 multiply_add_fusion
  49.1 1.3 select_reduce_fusion.2
  50.4 55.7 %all-gather.2.cloned.1.call-done = bf16[32,224,256]{2,1,0:T(8,128)(2,1)} async-done(((bf16[2,224,256]{2,1,0:T(8,128)(2,1)}), bf16[32,224,256]{2,1,0:T(8,128)(2,1)}) %all-gather.2.cloned.1.call-update) | async-done | bytes 3670032 | tf_op jit(solution)/shard_map/all_gather | solution.py:53
  106.2 4.3 fusion.6
  110.4 4.4 multiply_reduce_fusion
  114.9 61.7 %pmax.7 = f32[6,224]{1,0:T(8,128)S(1)} all-reduce(f32[6,224]{1,0:T(8,128)S(1)} %get-tuple-element.17), channel_id=1, replica_groups=mesh['rec'=16,'frame'=32] {'frame'}, use_global_device_ids=true, to_apply=%region_6.0 | all-reduce | flops 1344 | bytes 10752 | tf_op jit(solution)/shard_map/pmax | solution.py:65
  176.5 4.9 fusion.13
  181.4 2.1 copy.23
  183.5 0.2 reduce-scatter.3.cloned.1.call-start
  183.7 0.7 add_rsqrt_fusion.1
  184.4 163.1 %all-reduce.5.cloned.1.call-done = f32[6,224,256]{2,0,1:T(8,128)} async-done(((f32[6,224,256]{2,0,1:T(8,128)}), f32[6,224,256]{2,0,1:T(8,128)}) %all-reduce.5.cloned.1.call-update) | async-done | bytes 1376272 | tf_op jit(solution)/shard_map/psum | solution.py:74
  347.5 1.9 multiply_reduce_fusion.1
  349.4 2.4 multiply_reduce_fusion.2
  351.8 1.4 fusion.44
  353.2 1.8 convert_multiply_fusion
  355.0 4.9 multiply_convert_fusion
  360.0 1.3 fusion.10
  361.3 0.7 copy-done.10
  362.0 2.1 copy.47
  364.0 1.3 dynamic-slice
  366.0 0.7 constant_dynamic-slice_fusion
  366.7 0.7 constant_dynamic-slice_fusion.1
  367.4 5.7 convolution_bitcast_fusion
  373.1 2.3 fusion.5
  375.4 207.6 %reduce-scatter.3.cloned.1.call-done = f32[7,6,256]{2,1,0:T(8,128)} async-done(((f32[224,6,256]{2,1,0:T(8,128)}), f32[7,6,256]{2,1,0:T(8,128)}) %reduce-scatter.3.cloned.1.call-update) | async-done | bytes 43024 | tf_op jit(solution)/shard_map/reduce_scatter | solution.py:89
  583.0 1.3 fusion.27
  584.3 51.2 %all-reduce.6 = (f32[]{:T(128)}, bf16[32,7,256]{2,0,1:T(8,128)(2,1)S(1)}) all-reduce(f32[]{:T(128)} %get-tuple-element.14, f32[32,7,256]{2,0,1:T(8,128)S(1)} %fusion.27), channel_id=1, replica_groups=mesh['rec'=16,'frame'=32] {'rec'}, use_global_device_ids=true, to_apply=%region_11.12 | all-reduce | flops 57345 | bytes 344072 | tf_op jit(solution)/shard_map/psum | solution.py:111
  635.5 0.6 dynamic-slice_convert_fusion
  (30 shorter events, 0.2 us)
Async XLA Ops:
  7.2 103.2 %copy-start = (bf16[1,1536,256]{2,1,0:T(8,128)(2,1)S(1)}, bf16[1,1536,256]{2,1,0:T(8,128)(2,1)}, u32[]{:S(2)}) copy-start(bf16[1,1536,256]{2,1,0:T(8,128)(2,1)} %param.5) | copy-start | bytes 2359300
  7.2 99.0 %all-gather.2.cloned.1.call-start = ((), (), s32[]{:S(2)}) async-start(), calls=%async_computation.1 | async-start | bytes 3899392 | tf_op jit(solution)/shard_map/all_gather | solution.py:53
  46.8 300.7 %all-reduce.5.cloned.1.call-start = ((), (), s32[]{:S(2)}) async-start(), calls=%async_computation.2 | async-start | bytes 3670016 | tf_op jit(solution)/shard_map/psum | solution.py:74
  50.4 55.8 %copy-start.9 = (s32[6]{0:T(128)}, s32[6]{0:T(128)S(1)}, u32[]{:S(2)}) copy-start(s32[6]{0:T(128)S(1)} %get-tuple-element.7) | copy-start | bytes 76
  50.4 60.0 %copy-start.4 = (s32[6]{0:T(128)}, s32[6]{0:T(128)S(1)}, u32[]{:S(2)}) copy-start(s32[6]{0:T(128)S(1)} %get-tuple-element.6) | copy-start | bytes 76
  50.4 60.0 %copy-start.8 = (pred[6]{0:T(512)(128)(4,1)}, pred[6]{0:T(512)(128)(4,1)S(1)}, u32[]{:S(2)}) copy-start(pred[6]{0:T(512)(128)(4,1)S(1)} %broadcast_compare_fusion) | copy-start | bytes 22
  183.5 399.5 %reduce-scatter.3.cloned.1.call-start = ((), (), s32[]{:S(2)}) async-start(), calls=%async_computation.3 | async-start | bytes 1892352 | tf_op jit(solution)/shard_map/reduce_scatter | solution.py:89
  347.5 5.7 copy-start.1
  351.8 3.2 copy-start.3
  353.2 6.8 %copy-start.6 = (f32[6]{0:T(128)}, f32[6]{0:T(128)S(1)}, u32[]{:S(2)}) copy-start(f32[6]{0:T(128)S(1)} %get-tuple-element.13) | copy-start | bytes 76
  355.0 5.0 copy-start.2
  360.0 2.0 copy-start.10
  367.4 5.7 copy-start.11
  373.1 209.9 %copy-start.5 = (s32[6]{0:T(128)S(1)}, s32[6]{0:T(128)}, u32[]{:S(2)}) copy-start(s32[6]{0:T(128)} %copy-done.4) | copy-start | bytes 76
  373.1 209.9 %copy-start.7 = (f32[6]{0:T(128)S(1)}, f32[6]{0:T(128)}, u32[]{:S(2)}) copy-start(f32[6]{0:T(128)} %copy-done.6) | copy-start | bytes 76
Sparse Core Ops, SparseCore 0:
  46.9 59.1 all-gather.1
  183.6 163.8 all-reduce.4
  364.2 218.7 reduce-scatter.2
where the time goes:
time: 645 us; the launch traced here: 643 us
  waiting for transfers between devices  426 us (66%)
  blocking collectives  152 us (24%)
  matrix products  29 us (4%)
  between operations  14.6 us (2%)
  other arithmetic  11.7 us (2%)
  local copies, waits for them, and re-layouts  8.88 us (1%)
    reduce_scatter x1, waiting for transfers between devices, body(): lax.psum_scatter(jnp.einsum('slf,fd->lsd', score_gradient, upstream_signa...  208 us
    psum x1, waiting for transfers between devices, body(): context = lax.psum(value_partial, 'frame')  163 us
    pmax x1, blocking collectives, body(): row_max = lax.pmax(local_max, 'frame')  61.7 us
    all_gather x1, waiting for transfers between devices, body(): lax.all_gather(whole, 'rec', axis=0, tiled=True)  55.7 us
    psum x1, blocking collectives, body(): loss = lax.psum(jnp.sum(loss_part), 'rec')  51.2 us
    all_gather x1, blocking collectives, body(): whole = lax.all_gather(texts, 'frame', axis=1, tiled=True)  38.8 us
  transfers between devices with their start and end apart: 3, of which 3 were waited for; matrix products, arithmetic and copies ran while one was open for 2% of the time, Pallas kernels for 0%

commit v1 on v0

v1 whole, which is shorter than its diff:
```python
import jax
import jax.numpy as jnp
from jax import lax
from jax.experimental import pallas as pl
from jax.experimental.pallas import tpu as pltpu
from jax.sharding import PartitionSpec as P

EPS = 1e-06
TEMP = 10.0
BIAS = -1.0
LOSS_SCALE = 2048.0

X, Y = 4, 8
RECS = 16
OFFS = (1, 15, 8)
GROUPS = 3
D = 256
BLK = 16
COL = Y * BLK
ROWS = X * COL
TOKENS = 224
FR = 1536
SCALE = D**-0.5
MESH = pl.DeviceIdType.MESH
F32 = jnp.float32
BF16 = jnp.bfloat16

NT = (((1,), (1,)), ((), ()))
NN = (((1,), (0,)), ((), ()))
TN = (((0,), (0,)), ((), ()))


def dot(a, b, dims):
    return lax.dot_general(a, b, dims, preferred_element_type=F32)


def split_row(v, lane, row):
    hi = v.astype(BF16).astype(F32)
    rest = v - hi
    mid = rest.astype(BF16).astype(F32)
    low = rest - mid
    part = jnp.where(lane < 16, hi, jnp.where(lane < 32, mid, low))
    part = jnp.where((lane < 48) & ((lane & 15) == row), part, 0.0)
    return jnp.sum(part, axis=1, keepdims=True)


def kernel(
    rec_ref, text_ref, label_ref, frames_ref, texts_ref,
    loss_ref, gf_ref, gt_ref,
    own, q, w, s_s, m_o, m_i, t_o, t_i, m_t, part0, rsx_o, rsx_i, rsy_o, rsy_i, direct, uy, col_o, col_i, u, ds, dq0,
    dx_o, dx_i, dy_o, dy_i, back_o, back_i, gft, pad, gcos, loss_o, loss_i,
    s_text, r_text, s_st, r_st, s_back, r_back, s_loss, r_loss,
):
    r, f = lax.axis_index("rec"), lax.axis_index("frame")
    x, y = f // Y, f % Y

    def at_y(k):
        return (r, x * Y + lax.rem(y + k, Y))

    def at_x(k):
        return (r, lax.rem(x + k, X) * Y + y)

    def at_r(k):
        return (lax.rem(r + k, RECS), f)

    barrier = pltpu.get_barrier_semaphore()
    for k in range(1, RECS):
        pl.semaphore_signal(barrier, inc=1, device_id=at_r(k), device_id_type=MESH)
    for k in range(1, Y):
        pl.semaphore_signal(barrier, inc=1, device_id=at_y(k), device_id_type=MESH)
    for k in range(1, X):
        pl.semaphore_signal(barrier, inc=1, device_id=at_x(k), device_id_type=MESH)

    pad[...] = jnp.zeros_like(pad)
    pad[0:7, :] = texts_ref[0].astype(F32)
    pad[8:15, :] = texts_ref[1].astype(F32)
    own[...] = pad[...].astype(BF16)

    def count(p, c):
        rec = rec_ref[p, 0]
        text = text_ref[p]
        label = label_ref[p]
        hop = ((text >> 1) - rec) & (RECS - 1)
        mine = (rec == r).astype(jnp.int32)
        out = []
        for g in range(GROUPS):
            for s in range(2):
                hit = mine * (hop == OFFS[g]).astype(jnp.int32) * ((text & 1) == s).astype(jnp.int32)
                out.append(c[len(out)] + hit * label)
                out.append(c[len(out)] + hit * (1 - label))
        return tuple(out)

    counts = lax.fori_loop(0, 32, count, (jnp.int32(0),) * 12)

    pl.semaphore_wait(barrier, RECS - 1 + Y - 1 + X - 1)

    def send(src, dst, ss, rs, to):
        pltpu.make_async_remote_copy(src, dst, ss, rs, device_id=to, device_id_type=MESH).start()

    def wait(ref, sem):
        pltpu.make_async_copy(ref, ref, sem).wait()

    def gather_y(buf, g, st):
        for k in range(1, Y):
            send(buf.at[g, pl.ds(0, BLK)], buf.at[g, pl.ds(k * BLK, BLK)], s_st.at[st, g], r_st.at[st, g], at_y(k))

    def gather_x(buf, g, st):
        for k in range(1, X):
            send(buf.at[g, pl.ds(0, COL)], buf.at[g, pl.ds(k * COL, COL)], s_st.at[st, g], r_st.at[st, g], at_x(k))

    def scatter_x(out, into, g, k, st):
        send(out.at[g, k - 1], into.at[g, k - 1], s_st.at[st, g], r_st.at[st, g], at_x(X - k))

    def scatter_y(out, into, g, st):
        for k in range(1, Y):
            send(out.at[g, pl.ds(k * BLK - BLK, BLK)], into.at[g, pl.ds(k * BLK - BLK, BLK)], s_st.at[st, g], r_st.at[st, g], at_y(Y - k))

    for g in range(GROUPS):
        send(own, q.at[g, pl.ds(0, BLK)], s_text.at[g], r_text.at[g], at_r(RECS - OFFS[g]))

    def stage_a(g, c):
        wait(q.at[g, pl.ds(0, BLK)], r_text.at[g])
        gather_y(q, g, 0)
        return c

    lax.fori_loop(0, GROUPS, stage_a, 0)

    def stage_b(g, c):
        wait(q.at[g, pl.ds(BLK, COL - BLK)], r_st.at[0, g])
        gather_x(q, g, 1)
        return c

    lax.fori_loop(0, GROUPS, stage_b, 0)

    square = (COL, COL)
    diag = lax.broadcasted_iota(jnp.int32, square, 0) == lax.broadcasted_iota(jnp.int32, square, 1)

    def stage_c(g, c):
        def score(k):
            rows = pl.ds(k * COL, COL)
            s = dot(q[g, rows, :], frames_ref[0], NT) * SCALE
            s_s[g, rows, :] = s
            m = jnp.max(s, axis=1, keepdims=True)
            line = jnp.sum(jnp.where(diag, m, 0.0), axis=0, keepdims=True)
            m_o[g, pl.ds(k, 1), :] = line
            m_o[g, pl.ds(k + X, 1), :] = line

        score(0)
        wait(q.at[g, pl.ds(COL, ROWS - COL)], r_st.at[1, g])

        def one(k, c):
            score(k)
            return c

        lax.fori_loop(1, X, one, 0)
        for k in range(1, X):
            send(m_o.at[g], m_i.at[g, k - 1], s_st.at[2, g], r_st.at[2, g], at_x(k))
        return c

    lax.fori_loop(0, GROUPS, stage_c, 0)

    def stage_m(g, c):
        wait(m_i.at[g], r_st.at[2, g])
        top = m_o[g]
        for k in range(1, X):
            top = jnp.maximum(top, pltpu.roll(m_i[g, k - 1], k, 0))
        t_o[g] = top
        for k in range(1, Y):
            send(t_o.at[g], t_i.at[g, k - 1], s_st.at[3, g], r_st.at[3, g], at_y(k))
        return c

    lax.fori_loop(0, GROUPS, stage_m, 0)

    def stage_w(g, c):
        wait(t_i.at[g], r_st.at[3, g])
        top = t_o[g]
        for k in range(1, Y):
            top = jnp.maximum(top, pltpu.roll(t_i[g, k - 1], BLK * k, 1))
        m_t[g] = top

        def context(k):
            rows = pl.ds(k * COL, COL)
            m = jnp.sum(jnp.where(diag, m_t[g, pl.ds(k, 1), :], 0.0), axis=1, keepdims=True)
            wb = jnp.exp(s_s[g, rows, :] - m).astype(BF16)
            w[g, rows, :] = wb
            return dot(wb, frames_ref[0], NN)

        def one(k, c):
            rsx_o[g, k - 1] = context(k)
            scatter_x(rsx_o, rsx_i, g, k, 9)
            return c

        lax.fori_loop(1, X, one, 0)
        part0[g] = context(0)
        return c

    lax.fori_loop(0, GROUPS, stage_w, 0)

    def stage_d(g, c):
        wait(rsx_i.at[g], r_st.at[9, g])
        total = part0[g]
        for k in range(X - 1):
            total = total + rsx_i[g, k]
        part0[g, pl.ds(0, BLK), :] = total[:BLK]
        rsy_o[g] = total[BLK:]
        scatter_y(rsy_o, rsy_i, g, 10)
        return c

    lax.fori_loop(0, GROUPS, stage_d, 0)

    def stage_e(g, c):
        wait(rsy_i.at[g], r_st.at[10, g])
        qf = q[g, pl.ds(0, BLK), :].astype(F32).reshape(1, BLK, D)
        rest = rsy_i[g].reshape(Y - 1, BLK, D)
        ctx = part0[g, pl.ds(0, BLK), :].reshape(1, BLK, D) + jnp.sum(rest, axis=0, keepdims=True)
        lane = lax.broadcasted_iota(jnp.int32, (1, BLK, D), 2)
        row = lax.broadcasted_iota(jnp.int32, (1, BLK, D), 1)
        q_norm = lax.rsqrt(jnp.sum(qf * qf, axis=2, keepdims=True) + EPS)
        c_norm = lax.rsqrt(jnp.sum(ctx * ctx, axis=2, keepdims=True) + EPS)
        q_unit = qf * q_norm
        c_unit = ctx * c_norm
        cos = jnp.sum(q_unit * c_unit, axis=2, keepdims=True)
        d_ctx = (q_unit - cos * c_unit) * c_norm
        direct[g] = ((c_unit - cos * q_unit) * q_norm).reshape(BLK, D)
        d_ctx = jnp.where(row == 15, split_row(cos, lane, row), d_ctx).reshape(BLK, D)
        high = d_ctx.astype(BF16)
        uy[g, 0, 0:BLK, :] = high
        uy[g, 0, BLK:, :] = (d_ctx - high.astype(F32)).astype(BF16)
        for k in range(1, Y):
            send(uy.at[g, 0], uy.at[g, k], s_st.at[4, g], r_st.at[4, g], at_y(k))
        return c

    lax.fori_loop(0, GROUPS, stage_e, 0)

    def stage_f(g, c):
        wait(uy.at[g, pl.ds(1, Y - 1)], r_st.at[4, g])
        sums = jnp.sum(uy[g, :, 0:BLK, :].astype(F32)[:, 15, :128], axis=0, keepdims=True)
        col_o[g] = jnp.broadcast_to(sums, (8, 128))
        for k in range(1, X):
            send(col_o.at[g], col_i.at[g, k - 1], s_st.at[8, g], r_st.at[8, g], at_x(k))
        return c

    lax.fori_loop(0, GROUPS, stage_f, 0)

    loss = jnp.zeros((1, 128), F32)
    for g in range(GROUPS):
        wait(col_i.at[g], r_st.at[8, g])
        sums = col_o[g, 0:1, :] + col_i[g, 0, 0:1, :] + col_i[g, 1, 0:1, :] + col_i[g, 2, 0:1, :]
        lane = lax.broadcasted_iota(jnp.int32, (1, 128), 1)
        for s in range(2):
            pick = (lane < 48) & (((lane >> 3) & 1) == s) & ((lane & 7) < 7)
            score = jnp.sum(jnp.where(pick, sums, 0.0), axis=1, keepdims=True) * (1.0 / TOKENS)
            logit = jnp.broadcast_to(TEMP * score + BIAS, (1, 128))
            yes = counts[4 * g + 2 * s].astype(F32)
            no = counts[4 * g + 2 * s + 1].astype(F32)
            tail = jnp.log1p(jnp.exp(-jnp.abs(logit)))
            loss = loss + yes * (jnp.maximum(-logit, 0.0) + tail) + no * (jnp.maximum(logit, 0.0) + tail)
            pull = yes / (1.0 + jnp.exp(logit)) - no / (1.0 + jnp.exp(-logit))
            gcos[g, pl.ds(8 * s, 8), :] = jnp.broadcast_to(-LOSS_SCALE * TEMP / TOKENS * pull, (8, 128))
        row = lax.broadcasted_iota(jnp.int32, (Y, BLK, 1), 1)
        high = uy[g, :, 0:BLK, :].astype(F32)
        whole = (high + uy[g, :, BLK:, :].astype(F32)) * gcos[g, :, 0:1].reshape(1, BLK, 1)
        u[g, pl.ds(0, COL), :] = jnp.where((row & 7) < 7, whole, 0.0).reshape(COL, D).astype(BF16)
        gather_x(u, g, 5)

    loss_o[...] = jnp.broadcast_to(loss, (8, 128))
    for k in range(1, RECS):
        send(loss_o, loss_i.at[k - 1], s_loss, r_loss, at_r(k))

    for g in range(GROUPS):
        wait(u.at[g, pl.ds(COL, ROWS - COL)], r_st.at[5, g])

        def back(k, g=g):
            rows = pl.ds(k * COL, COL)
            dw = dot(u[g, rows, :], frames_ref[0], NT)
            d = (w[g, rows, :].astype(F32) * dw * SCALE).astype(BF16)
            ds[g, rows, :] = d
            return dot(d, frames_ref[0], NN)

        def one(k, c, g=g, back=back):
            dx_o[g, k - 1] = back(k).astype(BF16)
            scatter_x(dx_o, dx_i, g, k, 6)
            return c

        lax.fori_loop(1, X, one, 0)
        dq0[g] = back(0)

    def frame_grad(g):
        def tile(n, c):
            cols = pl.ds(pl.multiple_of(n * 512, 512), 512)
            acc = dot(q[g], ds[g, :, cols], TN) + dot(u[g], w[g, :, cols], TN)
            if g:
                acc = acc + gft[:, cols]
            if g < GROUPS - 1:
                gft[:, cols] = acc
            else:
                gf_ref[0, cols, :] = acc.T.astype(BF16)
            return c

        lax.fori_loop(0, FR // 512, tile, 0)

    def stage_h(g):
        wait(dx_i.at[g], r_st.at[6, g])
        total = dq0[g]
        for k in range(X - 1):
            total = total + dx_i[g, k].astype(F32)
        dq0[g] = total
        dy_o[g] = total[BLK:].astype(BF16)
        scatter_y(dy_o, dy_i, g, 7)

    def stage_i(g):
        wait(dy_i.at[g], r_st.at[7, g])
        total = dq0[g, pl.ds(0, BLK), :] + direct[g] * gcos[g, :, 0:1]
        total = total + jnp.sum(dy_i[g].astype(F32).reshape(Y - 1, BLK, D), axis=0)
        back_o[g] = total.astype(BF16)
        send(back_o.at[g], back_i.at[g], s_back.at[g], r_back.at[g], at_r(OFFS[g]))

    stage_h(0)
    stage_h(1)
    frame_grad(0)
    stage_h(2)
    stage_i(0)
    stage_i(1)
    frame_grad(1)
    stage_i(2)
    frame_grad(2)

    wait(loss_i, r_loss)
    loss_ref[0, 0] = jnp.sum(loss + jnp.sum(loss_i[:, 0, :], axis=0, keepdims=True)) * (1.0 / 128)

    total = None
    for g in range(GROUPS):
        wait(back_i.at[g], r_back.at[g])
        term = back_i[g].astype(F32)
        total = term if total is None else total + term
    gt_ref[0] = total[0:7].astype(BF16)
    gt_ref[1] = total[8:15].astype(BF16)

    for g in range(GROUPS):
        wait(own, s_text.at[g])
        wait(back_o.at[g], s_back.at[g])
        for st, ref in ((0, dy_i), (1, dx_i), (2, m_i), (3, t_i), (5, dx_i), (6, dx_i), (7, dy_i), (8, col_i), (9, rsx_i), (10, rsy_i)):
            wait(ref.at[g], s_st.at[st, g])
        wait(uy.at[g, pl.ds(1, Y - 1)], s_st.at[4, g])
    wait(loss_i, s_loss)


def body(frames, texts, pair_rec, pair_text, pair_label):
    vmem = pl.BlockSpec(memory_space=pltpu.VMEM)
    smem = pl.BlockSpec(memory_space=pltpu.SMEM)
    dma = pltpu.SemaphoreType.DMA
    v = pltpu.VMEM
    loss, gf, gt = pl.pallas_call(
        kernel,
        out_shape=(
            jax.ShapeDtypeStruct((1, 1), F32),
            jax.ShapeDtypeStruct((1, FR, D), BF16),
            jax.ShapeDtypeStruct((2, 7, D), BF16),
        ),
        in_specs=[smem, smem, smem, vmem, vmem],
        out_specs=(smem, vmem, vmem),
        scratch_shapes=[
            v((BLK, D), BF16),
            v((GROUPS, ROWS, D), BF16),
            v((GROUPS, ROWS, FR), BF16),
            v((GROUPS, ROWS, FR), F32),
            v((GROUPS, 8, 128), F32),
            v((GROUPS, X - 1, 8, 128), F32),
            v((GROUPS, 8, 128), F32),
            v((GROUPS, Y - 1, 8, 128), F32),
            v((GROUPS, 8, 128), F32),
            v((GROUPS, COL, D), F32),
            v((GROUPS, X - 1, COL, D), F32),
            v((GROUPS, X - 1, COL, D), F32),
            v((GROUPS, COL - BLK, D), F32),
            v((GROUPS, COL - BLK, D), F32),
            v((GROUPS, BLK, D), F32),
            v((GROUPS, Y, 2 * BLK, D), BF16),
            v((GROUPS, 8, 128), F32),
            v((GROUPS, X - 1, 8, 128), F32),
            v((GROUPS, ROWS, D), BF16),
            v((GROUPS, ROWS, FR), BF16),
            v((GROUPS, COL, D), F32),
            v((GROUPS, X - 1, COL, D), BF16),
            v((GROUPS, X - 1, COL, D), BF16),
            v((GROUPS, COL - BLK, D), BF16),
            v((GROUPS, COL - BLK, D), BF16),
            v((GROUPS, BLK, D), BF16),
            v((GROUPS, BLK, D), BF16),
            v((D, FR), F32),
            v((BLK, D), F32),
            v((GROUPS, BLK, 128), F32),
            v((8, 128), F32),
            v((RECS - 1, 8, 128), F32),
            dma((GROUPS,)), dma((GROUPS,)),
            dma((11, GROUPS)), dma((11, GROUPS)),
            dma((GROUPS,)), dma((GROUPS,)),
            dma, dma,
        ],
        compiler_params=pltpu.CompilerParams(
            collective_id=0, has_side_effects=True, vmem_limit_bytes=48 << 20
        ),
        cost_estimate=pl.CostEstimate(flops=7_300_000_000, bytes_accessed=1_700_000, transcendentals=2_400_000),
    )(pair_rec, pair_text, pair_label, frames, texts)
    return (loss.reshape(()), gf, gt)


def solution(mesh):
    return jax.shard_map(
        body,
        mesh=mesh,
        in_specs=(P("rec", "frame", None), P("rec", "frame", None), P(), P(), P()),
        out_specs=(P(), P("rec", "frame", None), P("rec", "frame", None)),
        check_vma=False,
    )
```

time: 645 us -> 108 us (0.17)
  waiting for transfers between devices: 426 us -> 0 us
  blocking collectives: 152 us -> 0 us
  Pallas kernels: 0 us -> 100 us
  matrix products: 29 us -> 0 us
  between operations: 14.6 us -> 2.41 us
  other arithmetic: 11.7 us -> 0 us
    reduce_scatter x1 -> x0, waiting for transfers between devices: 208 us -> none  [body(): lax.psum_scatter(jnp.einsum('slf,fd->lsd', score_gradient, upstream_signa...]
    psum x1 -> x0, waiting for transfers between devices: 163 us -> none  [body(): context = lax.psum(value_partial, 'frame')]
    pallas_call x0 -> x1, Pallas kernels: none -> 100 us  [body(): pl.pallas_call(kernel, out_shape=(jax.ShapeDtypeStruct((1, 1), F32), jax....]
    pmax x1 -> x0, blocking collectives: 61.7 us -> none  [body(): row_max = lax.pmax(local_max, 'frame')]
    all_gather x1 -> x0, waiting for transfers between devices: 55.7 us -> none  [body(): lax.all_gather(whole, 'rec', axis=0, tiled=True)]
    psum x1 -> x0, blocking collectives: 51.2 us -> none  [body(): loss = lax.psum(jnp.sum(loss_part), 'rec')]
    all_gather x1 -> x0, blocking collectives: 38.8 us -> none  [body(): whole = lax.all_gather(texts, 'frame', axis=1, tiled=True)]
    dot_general x8 -> x0, matrix products: 29 us -> none  [the longest x1 5.66 us: body(): jnp.einsum('cvm,cvz->mz', batch_weights, context_batch_gradient, preferre...]
  transfers between devices with their start and end apart: 3 -> 0, of which waited for: 3 -> 0; matrix products, arithmetic and copies ran while one was open for 2% -> 0% of each run, Pallas kernels for 0% -> 0%
where the time goes in v1:
time: 108 us; the launch traced here: 106 us
  Pallas kernels  100 us (93%)
  local copies, waits for them, and re-layouts  3.99 us (4%)
  between operations  2.41 us (2%)
    pallas_call x1, Pallas kernels, body(): pl.pallas_call(kernel, out_shape=(jax.ShapeDtypeStruct((1, 1), F32), jax....  100 us
    unnamed x12, local copies, waits for them, and re-layouts  3.99 us

profile of v1, /device:TPU:1, one launch (start us, length us, event | category | flops | bytes accessed | tf_op | source)
XLA Modules:
  0.0 106.4 jit_solution(11072787774902798126)
XLA Ops:
  0.6 0.0 copy-start.3
  0.6 0.7 copy.9.texts_ref
  1.3 0.0 copy-done.3
  1.3 0.0 copy-start.1
  1.3 0.0 copy-start.2
  1.4 0.1 copy.8.rec_ref
  1.4 0.6 copy-done.1
  2.0 0.0 copy-done.2
  2.0 0.0 copy-start
  2.0 1.1 %copy-done = bf16[1,1536,256]{2,1,0:T(8,128)(2,1)S(1)} copy-done((bf16[1,1536,256]{2,1,0:T(8,128)(2,1)S(1)}, bf16[1,1536,256]{2,1,0:T(8,128)(2,1)}, u32[]{:S(2)}) %copy-start) | copy-done | bytes 786456
  3.2 100.0 %shard_map.76 = (f32[1,1]{1,0:T(1,128)}, bf16[1,1536,256]{2,1,0:T(8,128)(2,1)S(1)}, bf16[2,7,256]{2,1,0:T(8,128)(2,1)S(1)}) custom-call(s32[32,1]{1,0:T(8,128)S(1)} %copy.8.rec_ref, s32[32]{0:T(128)S(1)} %copy-done.1, s32[32]{0:T(128)S(1)} %copy-done.2, bf16[1,1536,256]{2,1,0:T(8,128)(2,1)S(1)} %copy-done, bf16[2,7,256]{2,1,0:T(8,128)(2,1)S(1)} %copy.9.texts_ref), custom_call_target="tpu_custom_call" | custom-call | flops 7299999744 | bytes 1700000 | tf_op jit(solution)/shard_map/pallas_call | solution.py:353
  103.2 0.6 copy.10
  104.4 0.9 copy.14
Async XLA Ops:
  0.6 0.7 copy-start.3
  1.3 0.7 copy-start.1
  1.3 0.7 copy-start.2
  2.0 1.1 %copy-start = (bf16[1,1536,256]{2,1,0:T(8,128)(2,1)S(1)}, bf16[1,1536,256]{2,1,0:T(8,128)(2,1)}, u32[]{:S(2)}) copy-start(bf16[1,1536,256]{2,1,0:T(8,128)(2,1)} %frames_ref.1) | copy-start | bytes 2359300

commit v2 on v1

--- a/solution.py
+++ b/solution.py
@@ -16,6 +16,7 @@
 GROUPS = 3
 D = 256
 BLK = 16
+HALF = Y * BLK // 2
 COL = Y * BLK
 ROWS = X * COL
 TOKENS = 224
@@ -25,7 +26,6 @@
 F32 = jnp.float32
 BF16 = jnp.bfloat16
 
-NT = (((1,), (1,)), ((), ()))
 NN = (((1,), (0,)), ((), ()))
 TN = (((0,), (0,)), ((), ()))
 
@@ -45,11 +45,11 @@
 
 
 def kernel(
-    rec_ref, text_ref, label_ref, frames_ref, texts_ref,
+    rec_ref, text_ref, label_ref, frames_hbm, texts_ref,
     loss_ref, gf_ref, gt_ref,
-    own, q, w, s_s, m_o, m_i, t_o, t_i, m_t, part0, rsx_o, rsx_i, rsy_o, rsy_i, direct, uy, col_o, col_i, u, ds, dq0,
+    frames_ref, turned, own, q, w, s_s, m_o, m_i, t_o, t_i, m_t, part0, rsx_o, rsx_i, rsh, rsh_i, rsy_o, rsy_i, direct, uy, col_o, col_i, u, ds, dq0,
     dx_o, dx_i, dy_o, dy_i, back_o, back_i, gft, pad, gcos, loss_o, loss_i,
-    s_text, r_text, s_st, r_st, s_back, r_back, s_loss, r_loss,
+    s_frames, s_text, r_text, s_st, r_st, r_ax, r_h, s_back, r_back, s_loss, r_loss,
 ):
     r, f = lax.axis_index("rec"), lax.axis_index("frame")
     x, y = f // Y, f % Y
@@ -63,6 +63,8 @@
     def at_r(k):
         return (lax.rem(r + k, RECS), f)
 
+    load = pltpu.make_async_copy(frames_hbm.at[0], frames_ref, s_frames)
+    load.start()
     barrier = pltpu.get_barrier_semaphore()
     for k in range(1, RECS):
         pl.semaphore_signal(barrier, inc=1, device_id=at_r(k), device_id_type=MESH)
@@ -75,6 +77,54 @@
     pad[0:7, :] = texts_ref[0].astype(F32)
     pad[8:15, :] = texts_ref[1].astype(F32)
     own[...] = pad[...].astype(BF16)
+
+    pl.semaphore_wait(barrier, RECS - 1 + Y - 1 + X - 1)
+
+    def send(src, dst, ss, rs, to):
+        pltpu.make_async_remote_copy(src, dst, ss, rs, device_id=to, device_id_type=MESH).start()
+
+    def wait(ref, sem):
+        pltpu.make_async_copy(ref, ref, sem).wait()
+
+    def gather_y(buf, g, st):
+        for k in range(1, Y):
+            send(buf.at[g, pl.ds(0, BLK)], buf.at[g, pl.ds(k * BLK, BLK)], s_st.at[st, g], r_st.at[st, g], at_y(k))
+
+    def gather_x(buf, g, st, i):
+        send(buf.at[g, pl.ds(0, COL)], buf.at[g, pl.ds(COL, COL)], s_st.at[st, g], r_ax.at[i, g, 0], at_x(1))
+        send(buf.at[g, pl.ds(0, COL)], buf.at[g, pl.ds(3 * COL, COL)], s_st.at[st, g], r_ax.at[i, g, 1], at_x(3))
+
+    def forward_x(buf, g, st, i):
+        near, far, half = pl.ds(COL, HALF), pl.ds(3 * COL + HALF, HALF), 2 * COL + HALF
+        wait(buf.at[g, pl.ds(COL, COL)], r_ax.at[i, g, 0])
+        send(buf.at[g, near], buf.at[g, pl.ds(2 * COL, HALF)], s_st.at[st, g], r_ax.at[i, g, 2], at_x(1))
+        wait(buf.at[g, pl.ds(3 * COL, COL)], r_ax.at[i, g, 1])
+        send(buf.at[g, far], buf.at[g, pl.ds(half, HALF)], s_st.at[st, g], r_ax.at[i, g, 2], at_x(3))
+
+    def scatter_x(out, into, g, k, st):
+        send(out.at[g, k - 1], into.at[g, k - 1], s_st.at[st, g], r_st.at[st, g], at_x(X - k))
+
+    def scatter_far(out, halves, g, st, i):
+        send(out.at[g, 2, pl.ds(0, HALF)], halves.at[g, 0], s_st.at[st, g], r_h.at[i, g, 0], at_x(3))
+        send(out.at[g, 2, pl.ds(HALF, HALF)], halves.at[g, 1], s_st.at[st, g], r_h.at[i, g, 1], at_x(1))
+
+    def scatter_first(out, into, g, st, side):
+        rows = pl.ds(HALF - HALF * side, HALF)
+        send(out.at[g, side, rows], into.at[g, side, rows], s_st.at[st, g], r_st.at[st, g], at_x(3 - 2 * side))
+
+    def scatter_last(out, into, halves, mine, g, st, i):
+        for side in range(2):
+            rows = pl.ds(HALF * side, HALF)
+            wait(halves.at[g, side], r_h.at[i, g, side])
+            out[g, side, rows, :] = (mine[g, side] + halves[g, side].astype(F32)).astype(out.dtype)
+            send(out.at[g, side, rows], into.at[g, side, rows], s_st.at[st, g], r_st.at[st, g], at_x(3 - 2 * side))
+
+    def scatter_y(out, into, g, st):
+        for k in range(1, Y):
+            send(out.at[g, pl.ds(k * BLK - BLK, BLK)], into.at[g, pl.ds(k * BLK - BLK, BLK)], s_st.at[st, g], r_st.at[st, g], at_y(Y - k))
+
+    for g in range(GROUPS):
+        send(own, q.at[g, pl.ds(0, BLK)], s_text.at[g], r_text.at[g], at_r(RECS - OFFS[g]))
 
     def count(p, c):
         rec = rec_ref[p, 0]
@@ -92,31 +142,14 @@
 
     counts = lax.fori_loop(0, 32, count, (jnp.int32(0),) * 12)
 
-    pl.semaphore_wait(barrier, RECS - 1 + Y - 1 + X - 1)
-
-    def send(src, dst, ss, rs, to):
-        pltpu.make_async_remote_copy(src, dst, ss, rs, device_id=to, device_id_type=MESH).start()
-
-    def wait(ref, sem):
-        pltpu.make_async_copy(ref, ref, sem).wait()
-
-    def gather_y(buf, g, st):
-        for k in range(1, Y):
-            send(buf.at[g, pl.ds(0, BLK)], buf.at[g, pl.ds(k * BLK, BLK)], s_st.at[st, g], r_st.at[st, g], at_y(k))
-
-    def gather_x(buf, g, st):
-        for k in range(1, X):
-            send(buf.at[g, pl.ds(0, COL)], buf.at[g, pl.ds(k * COL, COL)], s_st.at[st, g], r_st.at[st, g], at_x(k))
-
-    def scatter_x(out, into, g, k, st):
-        send(out.at[g, k - 1], into.at[g, k - 1], s_st.at[st, g], r_st.at[st, g], at_x(X - k))
-
-    def scatter_y(out, into, g, st):
-        for k in range(1, Y):
-            send(out.at[g, pl.ds(k * BLK - BLK, BLK)], into.at[g, pl.ds(k * BLK - BLK, BLK)], s_st.at[st, g], r_st.at[st, g], at_y(Y - k))
-
-    for g in range(GROUPS):
-        send(own, q.at[g, pl.ds(0, BLK)], s_text.at[g], r_text.at[g], at_r(RECS - OFFS[g]))
+    load.wait()
+
+    def turn(n, c):
+        at = pl.ds(pl.multiple_of(n * 256, 256), 256)
+        turned[:, at] = frames_ref[at, :].T
+        return c
+
+    lax.fori_loop(0, FR // 256, turn, 0)
 
     def stage_a(g, c):
         wait(q.at[g, pl.ds(0, BLK)], r_text.at[g])
@@ -127,7 +160,7 @@
 
     def stage_b(g, c):
         wait(q.at[g, pl.ds(BLK, COL - BLK)], r_st.at[0, g])
-        gather_x(q, g, 1)
+        gather_x(q, g, 1, 0)
         return c
 
     lax.fori_loop(0, GROUPS, stage_b, 0)
@@ -138,25 +171,29 @@
     def stage_c(g, c):
         def score(k):
             rows = pl.ds(k * COL, COL)
-            s = dot(q[g, rows, :], frames_ref[0], NT) * SCALE
+            s = dot(q[g, rows, :], turned[...], NN) * SCALE
             s_s[g, rows, :] = s
             m = jnp.max(s, axis=1, keepdims=True)
             line = jnp.sum(jnp.where(diag, m, 0.0), axis=0, keepdims=True)
             m_o[g, pl.ds(k, 1), :] = line
             m_o[g, pl.ds(k + X, 1), :] = line
 
-        score(0)
-        wait(q.at[g, pl.ds(COL, ROWS - COL)], r_st.at[1, g])
+        @pl.when(g < GROUPS - 1)
+        def _():
+            forward_x(q, g + 1, 1, 0)
 
         def one(k, c):
-            score(k)
+            score(lax.rem(k, X))
             return c
 
-        lax.fori_loop(1, X, one, 0)
+        lax.fori_loop(3, 6, one, 0)
+        wait(q.at[g, pl.ds(2 * COL, COL)], r_ax.at[0, g, 2])
+        score(2)
         for k in range(1, X):
             send(m_o.at[g], m_i.at[g, k - 1], s_st.at[2, g], r_st.at[2, g], at_x(k))
         return c
 
+    forward_x(q, 0, 1, 0)
     lax.fori_loop(0, GROUPS, stage_c, 0)
 
     def stage_m(g, c):
@@ -183,24 +220,33 @@
             m = jnp.sum(jnp.where(diag, m_t[g, pl.ds(k, 1), :], 0.0), axis=1, keepdims=True)
             wb = jnp.exp(s_s[g, rows, :] - m).astype(BF16)
             w[g, rows, :] = wb
-            return dot(wb, frames_ref[0], NN)
-
-        def one(k, c):
-            rsx_o[g, k - 1] = context(k)
-            scatter_x(rsx_o, rsx_i, g, k, 9)
+            return dot(wb, frames_ref[...], NN)
+
+        rsx_o[g, 2] = context(2)
+        scatter_far(rsx_o, rsh_i, g, 9, 0)
+
+        def one(side, c):
+            value = context(1 + 2 * side)
+            rsx_o[g, side] = value
+            rsh[g, side] = rsx_o[g, side, pl.ds(HALF * side, HALF), :]
+            scatter_first(rsx_o, rsx_i, g, 9, side)
             return c
 
-        lax.fori_loop(1, X, one, 0)
+        lax.fori_loop(0, 2, one, 0)
         part0[g] = context(0)
+
+        @pl.when(g > 0)
+        def _():
+            scatter_last(rsx_o, rsx_i, rsh_i, rsh, g - 1, 9, 0)
+
         return c
 
     lax.fori_loop(0, GROUPS, stage_w, 0)
+    scatter_last(rsx_o, rsx_i, rsh_i, rsh, GROUPS - 1, 9, 0)
 
     def stage_d(g, c):
         wait(rsx_i.at[g], r_st.at[9, g])
-        total = part0[g]
-        for k in range(X - 1):
-            total = total + rsx_i[g, k]
+        total = part0[g] + rsx_i[g, 0] + rsx_i[g, 1]
         part0[g, pl.ds(0, BLK), :] = total[:BLK]
         rsy_o[g] = total[BLK:]
         scatter_y(rsy_o, rsy_i, g, 10)
@@ -261,29 +307,38 @@
         high = uy[g, :, 0:BLK, :].astype(F32)
         whole = (high + uy[g, :, BLK:, :].astype(F32)) * gcos[g, :, 0:1].reshape(1, BLK, 1)
         u[g, pl.ds(0, COL), :] = jnp.where((row & 7) < 7, whole, 0.0).reshape(COL, D).astype(BF16)
-        gather_x(u, g, 5)
+        gather_x(u, g, 5, 1)
 
     loss_o[...] = jnp.broadcast_to(loss, (8, 128))
     for k in range(1, RECS):
         send(loss_o, loss_i.at[k - 1], s_loss, r_loss, at_r(k))
 
-    for g in range(GROUPS):
-        wait(u.at[g, pl.ds(COL, ROWS - COL)], r_st.at[5, g])
-
-        def back(k, g=g):
+    forward_x(u, 0, 5, 1)
+
+    def stage_g(g, c):
+        @pl.when(g < GROUPS - 1)
+        def _():
+            forward_x(u, g + 1, 5, 1)
+
+        def back(k):
             rows = pl.ds(k * COL, COL)
-            dw = dot(u[g, rows, :], frames_ref[0], NT)
+            dw = dot(u[g, rows, :], turned[...], NN)
             d = (w[g, rows, :].astype(F32) * dw * SCALE).astype(BF16)
             ds[g, rows, :] = d
-            return dot(d, frames_ref[0], NN)
-
-        def one(k, c, g=g, back=back):
+            return dot(d, frames_ref[...], NN)
+
+        wait(u.at[g, pl.ds(2 * COL, COL)], r_ax.at[1, g, 2])
+
+        def one(k, c):
             dx_o[g, k - 1] = back(k).astype(BF16)
             scatter_x(dx_o, dx_i, g, k, 6)
             return c
 
         lax.fori_loop(1, X, one, 0)
         dq0[g] = back(0)
+        return c
+
+    lax.fori_loop(0, GROUPS, stage_g, 0)
 
     def frame_grad(g):
         def tile(n, c):
@@ -339,7 +394,7 @@
     for g in range(GROUPS):
         wait(own, s_text.at[g])
         wait(back_o.at[g], s_back.at[g])
-        for st, ref in ((0, dy_i), (1, dx_i), (2, m_i), (3, t_i), (5, dx_i), (6, dx_i), (7, dy_i), (8, col_i), (9, rsx_i), (10, rsy_i)):
+        for st, ref in ((0, dy_i), (1, dx_o), (2, m_i), (3, t_i), (5, dx_o), (6, dx_o), (7, dy_i), (8, col_i), (9, rsx_o), (10, rsy_i)):
             wait(ref.at[g], s_st.at[st, g])
         wait(uy.at[g, pl.ds(1, Y - 1)], s_st.at[4, g])
     wait(loss_i, s_loss)
@@ -357,9 +412,11 @@
             jax.ShapeDtypeStruct((1, FR, D), BF16),
             jax.ShapeDtypeStruct((2, 7, D), BF16),
         ),
-        in_specs=[smem, smem, smem, vmem, vmem],
+        in_specs=[smem, smem, smem, pl.BlockSpec(memory_space=pl.ANY), vmem],
         out_specs=(smem, vmem, vmem),
         scratch_shapes=[
+            v((FR, D), BF16),
+            v((D, FR), BF16),
             v((BLK, D), BF16),
             v((GROUPS, ROWS, D), BF16),
             v((GROUPS, ROWS, FR), BF16),
@@ -371,7 +428,9 @@
             v((GROUPS, 8, 128), F32),
             v((GROUPS, COL, D), F32),
             v((GROUPS, X - 1, COL, D), F32),
-            v((GROUPS, X - 1, COL, D), F32),
+            v((GROUPS, 2, COL, D), F32),
+            v((GROUPS, 2, HALF, D), F32),
+            v((GROUPS, 2, HALF, D), F32),
             v((GROUPS, COL - BLK, D), F32),
             v((GROUPS, COL - BLK, D), F32),
             v((GROUPS, BLK, D), F32),
@@ -392,8 +451,10 @@
             v((GROUPS, BLK, 128), F32),
             v((8, 128), F32),
             v((RECS - 1, 8, 128), F32),
+            dma,
             dma((GROUPS,)), dma((GROUPS,)),
             dma((11, GROUPS)), dma((11, GROUPS)),
+            dma((2, GROUPS, 3)), dma((1, GROUPS, 2)),
             dma((GROUPS,)), dma((GROUPS,)),
             dma, dma,
         ],

time: 108 us -> 106 us (0.981)
  the two profiles are of different devices: /device:TPU:1 before, /device:TPU:66 now
where the time goes in v2:
time: 106 us
  Pallas kernels  99.4 us (94%)
  local copies, waits for them, and re-layouts  3.99 us (4%)
  between operations  2.41 us (2%)
    pallas_call x1, Pallas kernels, body(): pl.pallas_call(kernel, out_shape=(jax.ShapeDtypeStruct((1, 1), F32), jax....  99.4 us
    unnamed x12, local copies, waits for them, and re-layouts  3.99 us

profile of v2, /device:TPU:66, one launch (start us, length us, event | category | flops | bytes accessed | tf_op | source)
XLA Modules:
  0.0 105.8 jit_solution(1635065585866978255)
XLA Ops:
  0.6 0.0 copy-start.3
  0.6 0.7 copy.9.texts_ref
  1.3 0.0 copy-done.3
  1.3 0.0 copy-start.1
  1.3 0.0 copy-start.2
  1.4 0.1 copy.8.rec_ref
  1.4 0.6 copy-done.1
  2.0 0.0 copy-done.2
  2.0 0.0 copy-start
  2.0 1.1 %copy-done = bf16[1,1536,256]{2,1,0:T(8,128)(2,1)S(1)} copy-done((bf16[1,1536,256]{2,1,0:T(8,128)(2,1)S(1)}, bf16[1,1536,256]{2,1,0:T(8,128)(2,1)}, u32[]{:S(2)}) %copy-start) | copy-done | bytes 786456
  3.2 99.4 %shard_map.76 = (f32[1,1]{1,0:T(1,128)}, bf16[1,1536,256]{2,1,0:T(8,128)(2,1)S(1)}, bf16[2,7,256]{2,1,0:T(8,128)(2,1)S(1)}) custom-call(s32[32,1]{1,0:T(8,128)S(1)} %copy.8.rec_ref, s32[32]{0:T(128)S(1)} %copy-done.1, s32[32]{0:T(128)S(1)} %copy-done.2, bf16[1,1536,256]{2,1,0:T(8,128)(2,1)S(1)} %copy-done, bf16[2,7,256]{2,1,0:T(8,128)(2,1)S(1)} %copy.9.texts_ref), custom_call_target="tpu_custom_call" | custom-call | flops 7299999744 | bytes 1700000 | tf_op jit(solution)/shard_map/pallas_call | solution.py:408
  102.6 0.6 copy.10
  103.8 0.9 copy.14
Async XLA Ops:
  0.6 0.7 copy-start.3
  1.3 0.7 copy-start.1
  1.3 0.7 copy-start.2
  2.0 1.1 %copy-start = (bf16[1,1536,256]{2,1,0:T(8,128)(2,1)S(1)}, bf16[1,1536,256]{2,1,0:T(8,128)(2,1)}, u32[]{:S(2)}) copy-start(bf16[1,1536,256]{2,1,0:T(8,128)(2,1)} %frames_hbm.1) | copy-start | bytes 2359300

commit v3 on v2

--- a/solution.py
+++ b/solution.py
@@ -1,3 +1,5 @@
+import functools
+
 import jax
 import jax.numpy as jnp
 from jax import lax
@@ -13,7 +15,7 @@
 X, Y = 4, 8
 RECS = 16
 OFFS = (1, 15, 8)
-GROUPS = 3
+OWNERS = 3
 D = 256
 BLK = 16
 HALF = Y * BLK // 2
@@ -45,9 +47,10 @@
 
 
 def kernel(
+    GROUPS,
     rec_ref, text_ref, label_ref, frames_hbm, texts_ref,
     loss_ref, gf_ref, gt_ref,
-    frames_ref, turned, own, q, w, s_s, m_o, m_i, t_o, t_i, m_t, part0, rsx_o, rsx_i, rsh, rsh_i, rsy_o, rsy_i, direct, uy, col_o, col_i, u, ds, dq0,
+    frames_ref, turned, own, texts_i, slots, q, w, s_s, m_o, m_i, t_o, t_i, m_t, part0, rsx_o, rsx_i, rsh, rsh_i, rsy_o, rsy_i, direct, uy, col_o, col_i, u, ds, dq0,
     dx_o, dx_i, dy_o, dy_i, back_o, back_i, gft, pad, gcos, loss_o, loss_i,
     s_frames, s_text, r_text, s_st, r_st, r_ax, r_h, s_back, r_back, s_loss, r_loss,
 ):
@@ -123,8 +126,8 @@
         for k in range(1, Y):
             send(out.at[g, pl.ds(k * BLK - BLK, BLK)], into.at[g, pl.ds(k * BLK - BLK, BLK)], s_st.at[st, g], r_st.at[st, g], at_y(Y - k))
 
-    for g in range(GROUPS):
-        send(own, q.at[g, pl.ds(0, BLK)], s_text.at[g], r_text.at[g], at_r(RECS - OFFS[g]))
+    for g in range(OWNERS):
+        send(own, texts_i.at[g], s_text.at[g], r_text.at[g], at_r(RECS - OFFS[g]))
 
     def count(p, c):
         rec = rec_ref[p, 0]
@@ -133,7 +136,7 @@
         hop = ((text >> 1) - rec) & (RECS - 1)
         mine = (rec == r).astype(jnp.int32)
         out = []
-        for g in range(GROUPS):
+        for g in range(OWNERS):
             for s in range(2):
                 hit = mine * (hop == OFFS[g]).astype(jnp.int32) * ((text & 1) == s).astype(jnp.int32)
                 out.append(c[len(out)] + hit * label)
@@ -142,6 +145,14 @@
 
     counts = lax.fori_loop(0, 32, count, (jnp.int32(0),) * 12)
 
+    picks, taken = [], jnp.int32(0)
+    for t in range(2 * OWNERS):
+        named = (counts[2 * t] + counts[2 * t + 1] > 0).astype(jnp.int32)
+        picks.append([(named * (taken == j).astype(jnp.int32)).astype(F32) for j in range(2 * GROUPS)])
+        taken = taken + named
+    slot_yes = [sum(picks[t][j] * counts[2 * t].astype(F32) for t in range(2 * OWNERS)) for j in range(2 * GROUPS)]
+    slot_no = [sum(picks[t][j] * counts[2 * t + 1].astype(F32) for t in range(2 * OWNERS)) for j in range(2 * GROUPS)]
+
     load.wait()
 
     def turn(n, c):
@@ -151,12 +162,15 @@
 
     lax.fori_loop(0, FR // 256, turn, 0)
 
-    def stage_a(g, c):
-        wait(q.at[g, pl.ds(0, BLK)], r_text.at[g])
+    texts = []
+    for g in range(OWNERS):
+        wait(texts_i.at[g], r_text.at[g])
+        both = texts_i[g].astype(F32)
+        texts += [both[:8], both[8:]]
+    for g in range(GROUPS):
+        mine = [sum(picks[t][2 * g + s] * texts[t] for t in range(2 * OWNERS)) for s in range(2)]
+        q[g, pl.ds(0, BLK), :] = jnp.concatenate(mine, axis=0).astype(BF16)
         gather_y(q, g, 0)
-        return c
-
-    lax.fori_loop(0, GROUPS, stage_a, 0)
 
     def stage_b(g, c):
         wait(q.at[g, pl.ds(BLK, COL - BLK)], r_st.at[0, g])
@@ -297,8 +311,7 @@
             pick = (lane < 48) & (((lane >> 3) & 1) == s) & ((lane & 7) < 7)
             score = jnp.sum(jnp.where(pick, sums, 0.0), axis=1, keepdims=True) * (1.0 / TOKENS)
             logit = jnp.broadcast_to(TEMP * score + BIAS, (1, 128))
-            yes = counts[4 * g + 2 * s].astype(F32)
-            no = counts[4 * g + 2 * s + 1].astype(F32)
+            yes, no = slot_yes[2 * g + s], slot_no[2 * g + s]
             tail = jnp.log1p(jnp.exp(-jnp.abs(logit)))
             loss = loss + yes * (jnp.maximum(-logit, 0.0) + tail) + no * (jnp.maximum(logit, 0.0) + tail)
             pull = yes / (1.0 + jnp.exp(logit)) - no / (1.0 + jnp.exp(-logit))
@@ -367,46 +380,56 @@
         wait(dy_i.at[g], r_st.at[7, g])
         total = dq0[g, pl.ds(0, BLK), :] + direct[g] * gcos[g, :, 0:1]
         total = total + jnp.sum(dy_i[g].astype(F32).reshape(Y - 1, BLK, D), axis=0)
-        back_o[g] = total.astype(BF16)
-        send(back_o.at[g], back_i.at[g], s_back.at[g], r_back.at[g], at_r(OFFS[g]))
-
-    stage_h(0)
-    stage_h(1)
+        slots[g] = total
+
+    def send_back():
+        for g in range(OWNERS):
+            mine = []
+            for t in (2 * g, 2 * g + 1):
+                mine.append(sum(picks[t][j] * slots[j // 2, 8 * (j % 2) : 8 * (j % 2) + 8, :] for j in range(2 * GROUPS)))
+            back_o[g] = jnp.concatenate(mine, axis=0).astype(BF16)
+            send(back_o.at[g], back_i.at[g], s_back.at[g], r_back.at[g], at_r(OFFS[g]))
+
+    for g in range(GROUPS - 1):
+        stage_h(g)
     frame_grad(0)
-    stage_h(2)
-    stage_i(0)
-    stage_i(1)
-    frame_grad(1)
-    stage_i(2)
-    frame_grad(2)
+    stage_h(GROUPS - 1)
+    for g in range(GROUPS - 1):
+        stage_i(g)
+    for g in range(1, GROUPS - 1):
+        frame_grad(g)
+    stage_i(GROUPS - 1)
+    send_back()
+    frame_grad(GROUPS - 1)
 
     wait(loss_i, r_loss)
     loss_ref[0, 0] = jnp.sum(loss + jnp.sum(loss_i[:, 0, :], axis=0, keepdims=True)) * (1.0 / 128)
 
     total = None
-    for g in range(GROUPS):
+    for g in range(OWNERS):
         wait(back_i.at[g], r_back.at[g])
         term = back_i[g].astype(F32)
         total = term if total is None else total + term
     gt_ref[0] = total[0:7].astype(BF16)
     gt_ref[1] = total[8:15].astype(BF16)
 
-    for g in range(GROUPS):
+    for g in range(OWNERS):
         wait(own, s_text.at[g])
         wait(back_o.at[g], s_back.at[g])
+    for g in range(GROUPS):
         for st, ref in ((0, dy_i), (1, dx_o), (2, m_i), (3, t_i), (5, dx_o), (6, dx_o), (7, dy_i), (8, col_i), (9, rsx_o), (10, rsy_i)):
             wait(ref.at[g], s_st.at[st, g])
         wait(uy.at[g, pl.ds(1, Y - 1)], s_st.at[4, g])
     wait(loss_i, s_loss)
 
 
-def body(frames, texts, pair_rec, pair_text, pair_label):
+def step(GROUPS, frames, texts, pair_rec, pair_text, pair_label):
     vmem = pl.BlockSpec(memory_space=pltpu.VMEM)
     smem = pl.BlockSpec(memory_space=pltpu.SMEM)
     dma = pltpu.SemaphoreType.DMA
     v = pltpu.VMEM
     loss, gf, gt = pl.pallas_call(
-        kernel,
+        functools.partial(kernel, GROUPS),
         out_shape=(
             jax.ShapeDtypeStruct((1, 1), F32),
             jax.ShapeDtypeStruct((1, FR, D), BF16),
@@ -418,6 +441,8 @@
             v((FR, D), BF16),
             v((D, FR), BF16),
             v((BLK, D), BF16),
+            v((OWNERS, BLK, D), BF16),
+            v((GROUPS, BLK, D), F32),
             v((GROUPS, ROWS, D), BF16),
             v((GROUPS, ROWS, FR), BF16),
             v((GROUPS, ROWS, FR), F32),
@@ -444,26 +469,37 @@
             v((GROUPS, X - 1, COL, D), BF16),
             v((GROUPS, COL - BLK, D), BF16),
             v((GROUPS, COL - BLK, D), BF16),
-            v((GROUPS, BLK, D), BF16),
-            v((GROUPS, BLK, D), BF16),
+            v((OWNERS, BLK, D), BF16),
+            v((OWNERS, BLK, D), BF16),
             v((D, FR), F32),
             v((BLK, D), F32),
             v((GROUPS, BLK, 128), F32),
             v((8, 128), F32),
             v((RECS - 1, 8, 128), F32),
             dma,
-            dma((GROUPS,)), dma((GROUPS,)),
+            dma((OWNERS,)), dma((OWNERS,)),
             dma((11, GROUPS)), dma((11, GROUPS)),
             dma((2, GROUPS, 3)), dma((1, GROUPS, 2)),
-            dma((GROUPS,)), dma((GROUPS,)),
+            dma((OWNERS,)), dma((OWNERS,)),
             dma, dma,
         ],
         compiler_params=pltpu.CompilerParams(
-            collective_id=0, has_side_effects=True, vmem_limit_bytes=48 << 20
+            collective_id=GROUPS, has_side_effects=True, vmem_limit_bytes=48 << 20
         ),
         cost_estimate=pl.CostEstimate(flops=7_300_000_000, bytes_accessed=1_700_000, transcendentals=2_400_000),
     )(pair_rec, pair_text, pair_label, frames, texts)
     return (loss.reshape(()), gf, gt)
+
+
+def body(frames, texts, pair_rec, pair_text, pair_label):
+    same = (pair_rec == jnp.arange(RECS)[None, :])[:, :, None] & (pair_text[:, None] == jnp.arange(2 * RECS)[None, :])[:, None, :]
+    named = jnp.sum(jnp.any(same, axis=0).astype(jnp.int32), axis=1)
+    return lax.cond(
+        jnp.max(named) <= 4,
+        functools.partial(step, 2),
+        functools.partial(step, 3),
+        frames, texts, pair_rec, pair_text, pair_label,
+    )
 
 
 def solution(mesh):

time: 106 us -> 95.8 us (0.904)
  the two profiles are of different devices: /device:TPU:66 before, /device:TPU:1 now
where the time goes in v3:
time: 95.8 us; the launch traced here: 95.7 us
  Pallas kernels  88.8 us (93%)
  between operations  3.04 us (3%)
  local copies, waits for them, and re-layouts  2.81 us (3%)
  other arithmetic  1.04 us (1%)
    pallas_call x1, Pallas kernels, step(): pl.pallas_call(functools.partial(kernel, GROUPS), out_shape=(jax.ShapeDty...  88.8 us
    unnamed x10, local copies, waits for them, and re-layouts  2.72 us

profile of v3, /device:TPU:1, one launch (start us, length us, event | category | flops | bytes accessed | tf_op | source)
XLA Modules:
  0.0 95.7 jit_solution(11271934685349010339)
XLA Ops:
  0.6 0.0 copy-start.1
  0.6 0.6 copy-done.1
  1.3 0.0 copy-start.2
  1.3 0.1 iota_compare_fusion.1
  1.4 0.6 copy-done.2
  1.9 0.1 iota_compare_fusion
  2.0 0.0 copy-start
  2.0 0.1 and_reduce_fusion
  2.2 0.1 convert_reduce_fusion
  2.3 0.6 reduce_max.9
  2.9 0.0 copy-start.3
  3.6 0.0 copy-done
  3.6 0.0 copy-done.3
  3.6 88.9 %conditional.1 = (bf16[1,1536,256]{2,1,0:T(8,128)(2,1)S(1)}, bf16[2,7,256]{2,1,0:T(8,128)(2,1)S(1)}, f32[]{:T(128)}) conditional(s32[]{:T(128)} %convert_element_type.7, (s32[32,1]{0,1:T(1,128)S(1)}, s32[32]{0:T(128)S(1)}, s32[32]{0:T(128)S(1)}, bf16[1,1536,256]{2,1,0:T(8,128)(2,1)}, bf16[2,7,256]{2,0,1:T(2,128)(2,1)S(1)}) %tuple.34, ...), branch_computations={%region_3.0_spmd, %region_4.0_spmd} | conditional | flops 7299999744 | bytes 1714616 | solution.py:497
  3.6 0.1 copy.23.rec_ref
  3.7 88.8 %branch_1_fun.1 = (f32[1,1]{1,0:T(1,128)}, bf16[1,1536,256]{2,1,0:T(8,128)(2,1)S(1)}, bf16[2,7,256]{2,1,0:T(8,128)(2,1)S(1)}) custom-call(s32[32,1]{1,0:T(8,128)S(1)} %copy.23.rec_ref, s32[32]{0:T(128)S(1)} %get-tuple-element.29.text_ref, s32[32]{0:T(128)S(1)} %get-tuple-element.47.label_ref, bf16[1,1536,256]{2,1,0:T(8,128)(2,1)} %get-tuple-element.49.frames_hbm, ...), custom_call_target="tpu_custom_call" | custom-call | flops 7299999744 | bytes 1700000 | tf_op jit(solution)/shard_map/cond/branch_1_fun/pallas_call | solution.py:431
  92.5 0.6 copy.25
  93.7 0.9 copy.35
  (1 shorter events, 0.0 us)
Async XLA Ops:
  0.6 0.7 copy-start.1
  1.3 0.7 copy-start.2
  2.0 1.6 %copy-start = (bf16[2,7,256]{2,0,1:T(2,128)(2,1)S(1)}, bf16[2,7,256]{2,0,1:T(2,128)(2,1)}, u32[]{:S(2)}) copy-start(bf16[2,7,256]{2,0,1:T(2,128)(2,1)} %param.8) | copy-start | bytes 21508
  2.9 0.7 copy-start.3
